TPU v7x, 32 devices: a whole 2x2x4 slice. The times are simulated.
32 devices in a mesh: fsdp: 16 (over z, x, core), tp: 2 (over y).
Axes of the slice: x: 2, y: 2, z: 4, core: 2. Of those that a mesh axis runs over, the one named last changes fastest.
Arguments:
- activations: bfloat16 [4096, 8192], P('fsdp'), may hold values from -6 to 6
- grad_output: bfloat16 [4096, 28672], P('fsdp', 'tp'), may hold values from -0.25 to 0.25
- projector: bfloat16 [8192, 1024], P('fsdp'), may hold values from -0.09375 to 0.09375
- first_moment: float32 [1024, 28672], P('fsdp', 'tp'), may hold values from -0.625 to 0.625
- second_moment: float32 [1024, 28672], P('fsdp', 'tp'), may hold values from 0.01 to 0.5
Outputs:
- new_first: float32 [1024, 28672], P('fsdp', 'tp')
- new_second: float32 [1024, 28672], P('fsdp', 'tp')
- weight_update: bfloat16 [8192, 28672], P('fsdp', 'tp')
All inputs are finite; a program needn't handle non-finite values.
Results may differ from a plain program's by a relative error of at most 0.0059.
Values may be sent and summed in bfloat16 or wider, within the bound.
A program may use at most 192 MiB of HBM per device.

v0:
```python
import jax
import jax.numpy as jnp
from jax import lax
from jax.sharding import PartitionSpec as P

first_fix = 0.9999734386011124
second_fix = 0.6339676587267705


def body(activations, grad_output, projector, first_moment, second_moment):
    rank_width = projector.shape[1]
    tp_count = lax.axis_size("tp")
    tp_place = lax.axis_index("tp")
    column_count = rank_width // tp_count
    spread = lax.all_to_all(activations, "fsdp", split_axis=1, concat_axis=0, tiled=True)
    proj_block = lax.dynamic_slice_in_dim(projector, tp_place * column_count, column_count, 1)
    partial_coords = lax.psum_scatter(
        jnp.dot(spread, proj_block, preferred_element_type=jnp.float32),
        "fsdp",
        scatter_dimension=0,
        tiled=True,
    ).astype(jnp.bfloat16)
    coords = lax.all_gather(partial_coords, "tp", axis=1, tiled=True)
    lowrank = lax.psum_scatter(
        lax.dot_general(
            coords, grad_output, (((0,), (0,)), ((), ())), preferred_element_type=jnp.float32
        ),
        "fsdp",
        scatter_dimension=0,
        tiled=True,
    )
    new_first = 0.9 * first_moment + 0.1 * lowrank
    new_second = 0.99 * second_moment + 0.01 * lowrank * lowrank
    direction = (new_first / first_fix / (jnp.sqrt(new_second / second_fix) + 1e-08)).astype(
        jnp.bfloat16
    )
    summed = jnp.dot(
        projector,
        lax.all_gather(direction, "fsdp", axis=0, tiled=True),
        preferred_element_type=jnp.float32,
    )
    return (new_first, new_second, summed.astype(jnp.bfloat16))


def solution(mesh):
    return jax.shard_map(
        body,
        mesh=mesh,
        in_specs=(
            P("fsdp", None),
            P("fsdp", "tp"),
            P("fsdp", None),
            P("fsdp", "tp"),
            P("fsdp", "tp"),
        ),
        out_specs=(P("fsdp", "tp"), P("fsdp", "tp"), P("fsdp", "tp")),
        check_vma=False,
    )
```

profile of v0, /device:TPU:0, one launch (start us, length us, event | category | flops | bytes accessed | tf_op | source)
XLA Modules:
  0.0 1008.8 jit_solution(8346109997468610627)
XLA Ops:
  7.2 0.0 copy-start
  7.2 6.5 copy.10
  13.6 7.4 all-to-all-start
  21.1 0.0 reduce-scatter.3.cloned.1.call-start
  21.1 77.6 %all-to-all-done = bf16[256,16,512]{0,2,1:T(8,128)(2,1)} async-done(((bf16[256,16,512]{0,2,1:T(8,128)(2,1)}), bf16[256,16,512]{0,2,1:T(8,128)(2,1)}, u32[]{:S(2)}, u32[]{:S(2)}) %all-to-all-start) | async-done | bytes 4194336 | tf_op jit(solution)/shard_map/all_to_all | solution.py:15
  98.7 6.5 copy.11
  105.2 0.0 copy-done
  105.2 8.0 convolution_bitcast_fusion
  113.2 0.0 reduce-scatter.3.cloned.1.call-update
  113.2 0.0 reduce-scatter.5.cloned.1.call-start
  113.3 119.9 %reduce-scatter.3.cloned.1.call-done = f32[256,512]{0,1:T(8,128)} async-done(((f32[4096,512]{0,1:T(8,128)}), f32[256,512]{0,1:T(8,128)}) %reduce-scatter.3.cloned.1.call-update) | async-done | bytes 524304 | tf_op jit(solution)/shard_map/reduce_scatter | solution.py:17
  233.2 1.1 convert_element_type.12
  234.3 8.8 all_gather.6
  243.0 24.1 %fusion.5 = f32[1024,14336]{1,0:T(8,128)} fusion(bf16[256,1024]{0,1:T(8,128)(2,1)S(1)} %all_gather.6, bf16[256,14336]{1,0:T(8,128)(2,1)} %param.6), kind=kOutput, calls=%fused_computation.9 | convolution fusion | flops 7516192768 | bytes 66584576 | tf_op jit(solution)/shard_map/dot_general | solution.py:25
  267.1 0.0 reduce-scatter.5.cloned.1.call-update
  267.1 0.2 all-gather.2.cloned.1.call-start
  267.4 537.3 %reduce-scatter.5.cloned.1.call-done = f32[64,14336]{1,0:T(8,128)} async-done(((f32[1024,14336]{1,0:T(8,128)}), f32[64,14336]{1,0:T(8,128)}) %reduce-scatter.5.cloned.1.call-update) | async-done | bytes 3670032 | tf_op jit(solution)/shard_map/reduce_scatter | solution.py:24
  804.7 7.6 divide_convert_fusion
  812.2 0.0 all-gather.2.cloned.1.call-update
  812.2 147.6 %all-gather.2.cloned.1.call-done = bf16[1024,14336]{1,0:T(8,128)(2,1)} async-done(((bf16[64,14336]{1,0:T(8,128)(2,1)}), bf16[1024,14336]{1,0:T(8,128)(2,1)}) %all-gather.2.cloned.1.call-update) | async-done | bytes 29360144 | tf_op jit(solution)/shard_map/all_gather | solution.py:39
  959.9 22.4 %fusion = bf16[512,14336]{0,1:T(8,128)(2,1)} fusion(bf16[1024,14336]{1,0:T(8,128)(2,1)} %all-gather.2.cloned.1.call-done, bf16[512,1024]{1,0:T(8,128)(2,1)S(1)} %copy-done), kind=kOutput, calls=%fused_computation.1 | convolution fusion | flops 15039725568 | bytes 45088768 | tf_op jit(solution)/shard_map/dot_general | solution.py:37
  982.2 0.0 copy-start.1
  982.2 20.0 %copy.12 = bf16[512,14336]{1,0:T(8,128)(2,1)} copy(bf16[512,14336]{0,1:T(8,128)(2,1)} %fusion) | data formatting | bytes 29360128
  1002.2 0.0 copy-done.1
Async XLA Ops:
  7.2 98.0 %copy-start = (bf16[512,1024]{1,0:T(8,128)(2,1)S(1)}, bf16[512,1024]{1,0:T(8,128)(2,1)}, u32[]{:S(2)}) copy-start(bf16[512,1024]{1,0:T(8,128)(2,1)} %param.7) | copy-start | bytes 3145732
  13.6 85.1 %all-to-all-start = ((bf16[256,16,512]{0,2,1:T(8,128)(2,1)}), bf16[256,16,512]{0,2,1:T(8,128)(2,1)}, u32[]{:S(2)}, u32[]{:S(2)}) async-start(bf16[256,16,512]{0,2,1:T(8,128)(2,1)} %bitcast.12), calls=%async_computation | async-start | bytes 8388608 | tf_op jit(solution)/shard_map/all_to_all | solution.py:15
  21.1 212.1 %reduce-scatter.3.cloned.1.call-start = ((), (), s32[]{:S(2)}) async-start(), calls=%async_computation.3 | async-start | bytes 8912896 | tf_op jit(solution)/shard_map/reduce_scatter | solution.py:17
  113.2 691.5 %reduce-scatter.5.cloned.1.call-start = ((), (), s32[]{:S(2)}) async-start(), calls=%async_computation.4 | async-start | bytes 62390272 | tf_op jit(solution)/shard_map/reduce_scatter | solution.py:24
  267.1 692.7 %all-gather.2.cloned.1.call-start = ((), (), s32[]{:S(2)}) async-start(), calls=%async_computation.5 | async-start | bytes 31195136 | tf_op jit(solution)/shard_map/all_gather | solution.py:39
  982.2 20.0 %copy-start.1 = (bf16[512,1024]{1,0:T(8,128)(2,1)S(1)}, bf16[512,1024]{1,0:T(8,128)(2,1)}, u32[]{:S(2)}) copy-start(bf16[512,1024]{1,0:T(8,128)(2,1)} %param.7) | copy-start | bytes 3145732
Sparse Core Ops, SparseCore 0:
  113.3 119.8 reduce-scatter.2
  267.3 537.3 reduce-scatter.4
  812.4 147.4 all-gather.1
where the time goes:
time: 1010 us
  waiting for transfers between devices  883 us (87%)
  matrix products  54.4 us (5%)
  local copies, waits for them, and re-layouts  32.9 us (3%)
  between operations  13.8 us (1%)
    reduce_scatter x1, waiting for transfers between devices, body(): lax.psum_scatter(lax.dot_general(coords, grad_output, (((0,), (0,)), ((),...  537 us
    all_gather x1, waiting for transfers between devices, body(): lax.all_gather(direction, 'fsdp', axis=0, tiled=True)  148 us
    reduce_scatter x1, waiting for transfers between devices, body(): lax.psum_scatter(jnp.dot(spread, proj_block, preferred_element_type=jnp.f...  120 us
    all_to_all x1, waiting for transfers between devices, body(): lax.all_to_all(activations, 'fsdp', split_axis=1, concat_axis=0, tiled=True)  77.6 us
    unnamed x6, local copies, waits for them, and re-layouts  26.5 us
    dot_general x1, matrix products, body(): lax.dot_general(coords, grad_output, (((0,), (0,)), ((), ())), preferred_...  24.1 us
    dot_general x1, matrix products, body(): jnp.dot(projector, lax.all_gather(direction, 'fsdp', axis=0, tiled=True),...  22.4 us
  transfers between devices with their start and end apart: 4, of which 4 were waited for; matrix products, arithmetic and copies ran while one was open for 0% of the time, Pallas kernels for 0%

commit v1 on v0

v1 whole, which is shorter than its diff:
```python
import functools

import jax
import jax.numpy as jnp
from jax import lax
from jax.experimental import pallas as pl
from jax.experimental.pallas import tpu as pltpu
from jax.sharding import PartitionSpec as P

first_fix = 0.9999734386011124
second_fix = 0.6339676587267705

MESH = pl.DeviceIdType.MESH
LINE = 4
CORES = 2
CHUNKS = 14
AHEAD = 4
LAG = 4


def reduce_kernel(
    coords_ref, grad_ref, first_ref, second_ref,
    new_first_ref, new_second_ref, direction_ref,
    coords_all, grads, partial, landed,
    coords_send, coords_recv, own_sem, grad_send, grad_recv, part_send, part_recv,
):
    plane = coords_all.shape[0]
    rows = first_ref.shape[0]
    half = first_ref.shape[1] // CORES
    width = half // CHUNKS
    me = lax.axis_index("fsdp")
    tp = lax.axis_index("tp")
    z = lax.div(me, plane)
    slot = lax.rem(me, plane)
    chip = lax.div(slot, CORES)
    core = lax.rem(slot, CORES)

    def in_plane(step):
        return lax.rem(slot + step, plane)

    def on_line(dz, dc):
        return lax.rem(z + dz, LINE), lax.rem(core + dc, CORES)

    line_peers = [(dz, dc) for dz in range(LINE) for dc in range(CORES) if dz or dc]

    def device(z_to, slot_to):
        return (z_to * plane + slot_to, tp)

    barrier = pltpu.get_barrier_semaphore()
    for step in range(1, plane):
        pl.semaphore_signal(barrier, inc=1, device_id=device(z, in_plane(step)), device_id_type=MESH)
    for dz, dc in line_peers:
        if dz:
            z_to, core_to = on_line(dz, dc)
            pl.semaphore_signal(
                barrier, inc=1, device_id=device(z_to, chip * CORES + core_to), device_id_type=MESH
            )
    pl.semaphore_wait(barrier, plane - 1 + (LINE - 1) * CORES)

    def coords_copy(step):
        to = in_plane(step)
        return pltpu.make_async_remote_copy(
            src_ref=coords_ref.at[lax.div(to, CORES)],
            dst_ref=coords_all.at[slot],
            send_sem=coords_send.at[step - 1],
            recv_sem=coords_recv.at[slot],
            device_id=device(z, to),
            device_id_type=MESH,
        )

    def grad_copy(step, i):
        to = in_plane(step)
        start = pl.multiple_of(lax.rem(to, CORES) * half + i * width, 128)
        return pltpu.make_async_remote_copy(
            src_ref=grad_ref.at[:, pl.ds(start, width)],
            dst_ref=grads.at[slot, i],
            send_sem=grad_send.at[step - 1, i],
            recv_sem=grad_recv.at[slot, i],
            device_id=device(z, to),
            device_id_type=MESH,
        )

    def own_copy(i):
        start = pl.multiple_of(core * half + i * width, 128)
        return pltpu.make_async_copy(
            grad_ref.at[:, pl.ds(start, width)], grads.at[slot, i], own_sem.at[i]
        )

    def part_copy(index, i):
        z_to, core_to = on_line(*line_peers[index])
        return pltpu.make_async_remote_copy(
            src_ref=partial.at[z_to * CORES + core_to, i],
            dst_ref=landed.at[core, z, i],
            send_sem=part_send.at[index, i],
            recv_sem=part_recv.at[core, z, i],
            device_id=device(z_to, chip * CORES + core_to),
            device_id_type=MESH,
        )

    def arrived(ref, sem):
        pltpu.make_async_copy(ref, ref, sem).wait()

    def send_grads(i):
        own_copy(i).start()
        for step in range(1, plane):
            grad_copy(step, i).start()

    for step in range(1, plane):
        coords_copy(step).start()
    for i in range(AHEAD):
        send_grads(i)
    coords_all[slot] = coords_ref[chip]
    for step in range(1, plane):
        source = in_plane(step)
        arrived(coords_all.at[source], coords_recv.at[source])

    def multiply(i):
        own_copy(i).wait()
        for step in range(1, plane):
            source = in_plane(step)
            arrived(grads.at[source, i], grad_recv.at[source, i])
        total = jnp.dot(coords_all[0], grads[0, i], preferred_element_type=jnp.float32)
        for source in range(1, plane):
            total += jnp.dot(
                coords_all[source], grads[source, i], preferred_element_type=jnp.float32
            )
        total = total.astype(jnp.bfloat16)
        for block in range(LINE * CORES):
            partial[block, i] = total[block * rows : (block + 1) * rows]
        for index in range(len(line_peers)):
            part_copy(index, i).start()
        landed[core, z, i] = partial[z * CORES + core, i]

    def adam(i):
        for dz, dc in line_peers:
            z_from, core_from = on_line(dz, dc)
            arrived(landed.at[core_from, z_from, i], part_recv.at[core_from, z_from, i])
        for side in range(CORES):
            lowrank = landed[side, 0, i].astype(jnp.float32)
            for z_from in range(1, LINE):
                lowrank += landed[side, z_from, i].astype(jnp.float32)
            columns = pl.ds(pl.multiple_of(side * half + i * width, 128), width)
            new_first = 0.9 * first_ref[:, columns] + 0.1 * lowrank
            new_second = 0.99 * second_ref[:, columns] + 0.01 * lowrank * lowrank
            new_first_ref[:, columns] = new_first
            new_second_ref[:, columns] = new_second
            direction_ref[:, columns] = (
                new_first / first_fix / (jnp.sqrt(new_second / second_fix) + 1e-08)
            ).astype(jnp.bfloat16)

    @pl.loop(0, CHUNKS)
    def _(i):
        @pl.when(i + AHEAD < CHUNKS)
        def _():
            send_grads(i + AHEAD)

        multiply(i)

        @pl.when(i >= LAG)
        def _():
            adam(i - LAG)

    @pl.loop(CHUNKS - LAG, CHUNKS)
    def _(i):
        adam(i)

    for step in range(1, plane):
        coords_copy(step).wait_send()

    @pl.loop(0, CHUNKS)
    def _(i):
        for step in range(1, plane):
            grad_copy(step, i).wait_send()
        for index in range(len(line_peers)):
            part_copy(index, i).wait_send()


def reduced(coords, grad_output, first_moment, second_moment):
    chips, share, tokens = coords.shape
    plane = chips * CORES
    rows, columns = first_moment.shape
    width = columns // CORES // CHUNKS
    peers = LINE * CORES - 1
    vmem = pl.BlockSpec(memory_space=pltpu.VMEM)
    return pl.pallas_call(
        reduce_kernel,
        out_shape=(
            jax.ShapeDtypeStruct((rows, columns), jnp.float32),
            jax.ShapeDtypeStruct((rows, columns), jnp.float32),
            jax.ShapeDtypeStruct((rows, columns), jnp.bfloat16),
        ),
        in_specs=[vmem, pl.BlockSpec(memory_space=pl.ANY), vmem, vmem],
        out_specs=(vmem, vmem, vmem),
        scratch_shapes=[
            pltpu.VMEM((plane, share, tokens), jnp.bfloat16),
            pltpu.VMEM((plane, CHUNKS, tokens, width), jnp.bfloat16),
            pltpu.VMEM((LINE * CORES, CHUNKS, rows, width), jnp.bfloat16),
            pltpu.VMEM((CORES, LINE, CHUNKS, rows, width), jnp.bfloat16),
            pltpu.SemaphoreType.DMA((plane - 1,)),
            pltpu.SemaphoreType.DMA((plane,)),
            pltpu.SemaphoreType.DMA((CHUNKS,)),
            pltpu.SemaphoreType.DMA((plane - 1, CHUNKS)),
            pltpu.SemaphoreType.DMA((plane, CHUNKS)),
            pltpu.SemaphoreType.DMA((peers, CHUNKS)),
            pltpu.SemaphoreType.DMA((CORES, LINE, CHUNKS)),
        ],
        compiler_params=pltpu.CompilerParams(
            collective_id=0, has_side_effects=True, vmem_limit_bytes=58 * 2**20
        ),
        name="reduce_and_step",
    )(coords, grad_output, first_moment, second_moment)


def update_kernel(projector_ref, direction_ref, out_ref):
    out_ref[...] = jnp.dot(
        projector_ref[...], direction_ref[...], preferred_element_type=jnp.float32
    ).astype(jnp.bfloat16)


def back_projected(projector, direction):
    rows, rank = projector.shape
    columns = direction.shape[1]
    width = columns // CHUNKS
    return pl.pallas_call(
        update_kernel,
        out_shape=jax.ShapeDtypeStruct((rows, columns), jnp.bfloat16),
        grid=(CHUNKS,),
        in_specs=[
            pl.BlockSpec((rows, rank), lambda i: (0, 0)),
            pl.BlockSpec((rank, width), lambda i: (0, i)),
        ],
        out_specs=pl.BlockSpec((rows, width), lambda i: (0, i)),
        compiler_params=pltpu.CompilerParams(vmem_limit_bytes=40 * 2**20),
        name="back_project",
    )(projector, direction)


def body(activations, grad_output, projector, first_moment, second_moment):
    rank_width = projector.shape[1]
    tp_count = lax.axis_size("tp")
    tp_place = lax.axis_index("tp")
    chips = lax.axis_size("fsdp") // (LINE * CORES)
    column_count = rank_width // tp_count
    proj_block = lax.dynamic_slice_in_dim(projector, tp_place * column_count, column_count, 1)
    proj_all = lax.all_gather(proj_block, "fsdp", axis=0, tiled=True)
    coords_block = lax.dot_general(
        proj_all, activations, (((0,), (1,)), ((), ())), preferred_element_type=jnp.float32
    ).astype(jnp.bfloat16)
    coords = lax.all_gather(coords_block, "tp", axis=0, tiled=True)
    tokens = coords.shape[1]
    coords = coords.reshape(LINE, chips, -1, tokens).transpose(1, 0, 2, 3)
    coords = coords.reshape(chips, rank_width // chips, tokens)
    new_first, new_second, direction = reduced(coords, grad_output, first_moment, second_moment)
    direction_all = lax.all_gather(direction, "fsdp", axis=0, tiled=True)
    return (new_first, new_second, back_projected(projector, direction_all))


def solution(mesh):
    return jax.shard_map(
        body,
        mesh=mesh,
        in_specs=(
            P("fsdp", None),
            P("fsdp", "tp"),
            P("fsdp", None),
            P("fsdp", "tp"),
            P("fsdp", "tp"),
        ),
        out_specs=(P("fsdp", "tp"), P("fsdp", "tp"), P("fsdp", "tp")),
        check_vma=False,
    )
```

time: 1010 us -> 483 us (0.48)
  waiting for transfers between devices: 883 us -> 228 us
  Pallas kernels: 0 us -> 216 us
  matrix products: 54.4 us -> 6.94 us
  local copies, waits for them, and re-layouts: 32.9 us -> 7.91 us
    reduce_scatter x2 -> x0, waiting for transfers between devices: 657 us -> none  [the longest x1 537 us: body(): lax.psum_scatter(lax.dot_general(coords, grad_output, (((0,), (0,)), ((),...]
    pallas_call x0 -> x2, Pallas kernels: none -> 216 us  [the longest x1 191 us: reduced(): pl.pallas_call(reduce_kernel, out_shape=(jax.ShapeDtypeStruct((rows, colu...]
    all_gather x1 -> x2, waiting for transfers between devices: 148 us -> 228 us  [the longest x1 149 us: body(): direction_all = lax.all_gather(direction, 'fsdp', axis=0, tiled=True)]
    all_to_all x1 -> x0, waiting for transfers between devices: 77.6 us -> none  [body(): lax.all_to_all(activations, 'fsdp', split_axis=1, concat_axis=0, tiled=True)]
    dot_general x3 -> x1, matrix products: 54.4 us -> 6.94 us  [body(): lax.dot_general(proj_all, activations, (((0,), (1,)), ((), ())), preferre...]
    unnamed x6 -> x8, local copies, waits for them, and re-layouts: 26.5 us -> 5.21 us
  transfers between devices with their start and end apart: 4 -> 2, of which waited for: 4 -> 2; matrix products, arithmetic and copies ran while one was open for 0% -> 0% of each run, Pallas kernels for 0% -> 0%
where the time goes in v1:
time: 483 us; the launch traced here: 482 us
  waiting for transfers between devices  228 us (47%)
  Pallas kernels  216 us (45%)
  between operations  14.1 us (3%)
  blocking collectives  9.15 us (2%)
  local copies, waits for them, and re-layouts  7.91 us (2%)
  matrix products  6.94 us (1%)
    pallas_call x1, Pallas kernels, reduced(): pl.pallas_call(reduce_kernel, out_shape=(jax.ShapeDtypeStruct((rows, colu...  191 us
    all_gather x1, waiting for transfers between devices, body(): direction_all = lax.all_gather(direction, 'fsdp', axis=0, tiled=True)  149 us
    all_gather x1, waiting for transfers between devices, body(): proj_all = lax.all_gather(proj_block, 'fsdp', axis=0, tiled=True)  79.2 us
    pallas_call x1, Pallas kernels, back_projected(): pl.pallas_call(update_kernel, out_shape=jax.ShapeDtypeStruct((rows, colum...  25.4 us
  transfers between devices with their start and end apart: 2, of which 2 were waited for; matrix products, arithmetic and copies ran while one was open for 0% of the time, Pallas kernels for 0%

profile of v1, /device:TPU:0, one launch (start us, length us, event | category | flops | bytes accessed | tf_op | source)
XLA Modules:
  0.0 482.1 jit_solution(14912842549110793060)
XLA Ops:
  7.2 0.0 all-gather.3.cloned.1.call-start
  7.2 1.9 constant_dynamic-slice_fusion
  9.1 0.0 all-gather.3.cloned.1.call-update
  9.1 0.0 all-gather.5.cloned.1.call-start
  9.2 79.2 %all-gather.3.cloned.1.call-done = bf16[8192,512]{1,0:T(8,128)(2,1)} async-done(((bf16[512,512]{1,0:T(8,128)(2,1)}), bf16[8192,512]{1,0:T(8,128)(2,1)}) %all-gather.3.cloned.1.call-update) | async-done | bytes 8388624 | tf_op jit(solution)/shard_map/all_gather | solution.py:245
  88.4 6.9 %convolution_convert_fusion = bf16[512,256]{1,0:T(8,128)(2,1)S(1)} fusion(bf16[8192,512]{1,0:T(8,128)(2,1)} %all-gather.3.cloned.1.call-done, bf16[256,8192]{1,0:T(8,128)(2,1)} %param.5), kind=kOutput, calls=%fused_computation | convolution fusion | flops 2147614720 | bytes 12845056 | tf_op jit(solution)/shard_map/dot_general | solution.py:246
  95.3 9.1 %all_gather.10 = bf16[1024,256]{1,0:T(8,128)(2,1)S(1)} all-gather(bf16[512,256]{1,0:T(8,128)(2,1)S(1)} %convolution_convert_fusion), channel_id=1, replica_groups=mesh['fsdp'=16,'tp'=2] {'tp'}, dimensions={0}, use_global_device_ids=true | all-gather | bytes 786432 | tf_op jit(solution)/shard_map/all_gather | solution.py:249
  104.5 0.8 copy.8
  105.3 0.0 copy-start
  105.3 190.6 %reduce_and_step.1 = (f32[64,14336]{1,0:T(8,128)}, f32[64,14336]{1,0:T(8,128)}, bf16[64,14336]{1,0:T(8,128)(2,1)}) custom-call(bf16[2,512,256]{2,1,0:T(8,128)(2,1)} %bitcast.7, bf16[256,14336]{1,0:T(8,128)(2,1)} %grad_ref.1, f32[64,14336]{1,0:T(8,128)} %first_ref.1, f32[64,14336]{1,0:T(8,128)} %second_ref.1), custom_call_target="tpu_custom_call" | custom-call | tf_op jit(solution)/shard_map/reduce_and_step/pallas_call | solution.py:185
  295.9 0.0 all-gather.5.cloned.1.call-update
  295.9 148.8 %all-gather.5.cloned.1.call-done.direction_ref = bf16[1024,14336]{1,0:T(8,128)(2,1)} async-done(((bf16[64,14336]{1,0:T(8,128)(2,1)}), bf16[1024,14336]{1,0:T(8,128)(2,1)}) %all-gather.5.cloned.1.call-update) | async-done | bytes 29360144 | tf_op jit(solution)/shard_map/all_gather | solution.py:254
  444.7 0.0 copy-done
  444.7 0.0 copy-start.2
  444.7 25.4 %back_project.1 = bf16[512,14336]{1,0:T(8,128)(2,1)} custom-call(bf16[512,1024]{1,0:T(8,128)(2,1)S(1)} %copy-done, bf16[1024,14336]{1,0:T(8,128)(2,1)} %all-gather.5.cloned.1.call-done.direction_ref), custom_call_target="tpu_custom_call" | custom-call | tf_op jit(solution)/shard_map/back_project/pallas_call | solution.py:224
  470.1 0.0 copy-done.2
  470.1 0.0 copy-start.1
  470.1 1.9 copy.11
  471.9 1.5 copy-done.1
  473.4 1.8 copy.12
Async XLA Ops:
  7.2 81.2 %all-gather.3.cloned.1.call-start = ((), (), s32[]{:S(2)}) async-start(), calls=%async_computation | async-start | bytes 8912896 | tf_op jit(solution)/shard_map/all_gather | solution.py:245
  9.1 435.6 %all-gather.5.cloned.1.call-start = ((), (), s32[]{:S(2)}) async-start(), calls=%async_computation.1 | async-start | bytes 31195136 | tf_op jit(solution)/shard_map/all_gather | solution.py:254
  105.3 339.4 %copy-start = (bf16[512,1024]{1,0:T(8,128)(2,1)S(1)}, bf16[512,1024]{1,0:T(8,128)(2,1)}, u32[]{:S(2)}) copy-start(bf16[512,1024]{1,0:T(8,128)(2,1)} %projector_ref.1) | copy-start | bytes 3145732
  444.7 25.4 %copy-start.2 = (f32[64,14336]{1,0:T(8,128)S(1)}, f32[64,14336]{1,0:T(8,128)}, u32[]{:S(2)}) copy-start(f32[64,14336]{1,0:T(8,128)} %get-tuple-element.12) | copy-start | bytes 11010052
  470.1 3.4 copy-start.1
Sparse Core Ops, SparseCore 0:
  10.7 77.5 all-gather.2
  296.0 148.5 all-gather.4

commit v2 on v1

--- a/solution.py
+++ b/solution.py
@@ -19,12 +19,17 @@
 
 
 def reduce_kernel(
-    coords_ref, grad_ref, first_ref, second_ref,
+    act_ref, proj_ref, grad_ref, first_ref, second_ref,
     new_first_ref, new_second_ref, direction_ref,
-    coords_all, grads, partial, landed,
+    proj_all, acts, acc, acc_in, coords, coords_all, grads, partial, landed,
+    line_send, line_recv, row_send, row_recv, act_sem, act_send, act_recv, acc_send, acc_recv,
     coords_send, coords_recv, own_sem, grad_send, grad_recv, part_send, part_recv,
 ):
-    plane = coords_all.shape[0]
+    plane = grads.shape[0]
+    chips = plane // CORES
+    tps = lax.axis_size("tp")
+    parts = coords.shape[0]
+    depth = proj_ref.shape[0]
     rows = first_ref.shape[0]
     half = first_ref.shape[1] // CORES
     width = half // CHUNKS
@@ -34,6 +39,7 @@
     slot = lax.rem(me, plane)
     chip = lax.div(slot, CORES)
     core = lax.rem(slot, CORES)
+    sibling = chip * CORES + 1 - core
 
     def in_plane(step):
         return lax.rem(slot + step, plane)
@@ -43,30 +49,102 @@
 
     line_peers = [(dz, dc) for dz in range(LINE) for dc in range(CORES) if dz or dc]
 
-    def device(z_to, slot_to):
-        return (z_to * plane + slot_to, tp)
+    def device(z_to, slot_to, dt=0):
+        return (z_to * plane + slot_to, lax.rem(tp + dt, tps) if dt else tp)
 
     barrier = pltpu.get_barrier_semaphore()
-    for step in range(1, plane):
-        pl.semaphore_signal(barrier, inc=1, device_id=device(z, in_plane(step)), device_id_type=MESH)
+    for step in range(plane):
+        for dt in range(tps):
+            if step or dt:
+                pl.semaphore_signal(
+                    barrier, inc=1, device_id=device(z, in_plane(step), dt), device_id_type=MESH
+                )
     for dz, dc in line_peers:
         if dz:
             z_to, core_to = on_line(dz, dc)
             pl.semaphore_signal(
                 barrier, inc=1, device_id=device(z_to, chip * CORES + core_to), device_id_type=MESH
             )
-    pl.semaphore_wait(barrier, plane - 1 + (LINE - 1) * CORES)
-
-    def coords_copy(step):
-        to = in_plane(step)
-        return pltpu.make_async_remote_copy(
-            src_ref=coords_ref.at[lax.div(to, CORES)],
-            dst_ref=coords_all.at[slot],
-            send_sem=coords_send.at[step - 1],
-            recv_sem=coords_recv.at[slot],
-            device_id=device(z, to),
-            device_id_type=MESH,
-        )
+    pl.semaphore_wait(barrier, plane * tps - 1 + (LINE - 1) * CORES)
+
+    def arrived(ref, sem):
+        pltpu.make_async_copy(ref, ref, sem).wait()
+
+    def line_copy(dz):
+        z_to, _ = on_line(dz, 0)
+        return pltpu.make_async_remote_copy(
+            src_ref=proj_ref,
+            dst_ref=proj_all.at[z * chips + chip],
+            send_sem=line_send.at[dz],
+            recv_sem=line_recv.at[z],
+            device_id=device(z_to, slot),
+            device_id_type=MESH,
+        )
+
+    def row_copy(dz, dx):
+        z_from, _ = on_line(dz, 0)
+        block = z_from * chips + chip
+        return pltpu.make_async_remote_copy(
+            src_ref=proj_all.at[block] if dz else proj_ref,
+            dst_ref=proj_all.at[block],
+            send_sem=row_send.at[dx, dz],
+            recv_sem=row_recv.at[block],
+            device_id=device(z, lax.rem(chip + dx, chips) * CORES + core),
+            device_id_type=MESH,
+        )
+
+    def act_columns(block, side):
+        return act_ref.at[:, pl.ds(pl.multiple_of((block * CORES + side) * depth, 128), depth)]
+
+    def act_own(block):
+        return pltpu.make_async_copy(act_columns(block, core), acts.at[block, 0], act_sem.at[block])
+
+    def act_copy(block):
+        return pltpu.make_async_remote_copy(
+            src_ref=act_columns(block, 1 - core),
+            dst_ref=acts.at[block, 1],
+            send_sem=act_send.at[block],
+            recv_sem=act_recv.at[block],
+            device_id=device(z, sibling),
+            device_id_type=MESH,
+        )
+
+    def acc_copy():
+        return pltpu.make_async_remote_copy(
+            src_ref=acc.at[1],
+            dst_ref=acc_in,
+            send_sem=acc_send,
+            recv_sem=acc_recv,
+            device_id=device(z, sibling),
+            device_id_type=MESH,
+        )
+
+    def coords_place(q):
+        place = tp * parts + q
+        return lax.rem(place, chips), lax.div(place, chips)
+
+    def coords_copy(q, dc, dt):
+        chip_to, block = coords_place(q)
+        return pltpu.make_async_remote_copy(
+            src_ref=coords.at[q],
+            dst_ref=coords_all.at[slot, block],
+            send_sem=coords_send.at[q, dc * tps + dt],
+            recv_sem=coords_recv.at[slot, block],
+            device_id=device(z, chip_to * CORES + lax.rem(core + dc, CORES), dt),
+            device_id_type=MESH,
+        )
+
+    def each_coords_copy(act):
+        for q in range(parts):
+            chip_to, _ = coords_place(q)
+            for dc in range(CORES):
+                for dt in range(tps):
+                    if dc or dt:
+                        act(coords_copy(q, dc, dt))
+                    else:
+                        @pl.when(chip_to != chip)
+                        def _():
+                            act(coords_copy(q, 0, 0))
 
     def grad_copy(step, i):
         to = in_plane(step)
@@ -97,33 +175,78 @@
             device_id_type=MESH,
         )
 
-    def arrived(ref, sem):
-        pltpu.make_async_copy(ref, ref, sem).wait()
-
     def send_grads(i):
         own_copy(i).start()
         for step in range(1, plane):
             grad_copy(step, i).start()
 
-    for step in range(1, plane):
-        coords_copy(step).start()
-    for i in range(AHEAD):
-        send_grads(i)
-    coords_all[slot] = coords_ref[chip]
-    for step in range(1, plane):
+    blocks = acts.shape[0]
+    for dz in range(1, LINE):
+        line_copy(dz).start()
+    for dx in range(1, chips):
+        row_copy(0, dx).start()
+    for block in range(blocks):
+        act_own(block).start()
+        act_copy(block).start()
+    send_grads(0)
+    acc[...] = jnp.zeros_like(acc)
+
+    def accumulate(block, features):
+        act_own(block).wait()
+        arrived(acts.at[block, 1], act_recv.at[block])
+        tokens = acts.shape[2]
+        both = acts[block].reshape(CORES * tokens, depth)
+        acc[...] += jnp.dot(both, features, preferred_element_type=jnp.float32).reshape(acc.shape)
+
+    for dz in range(LINE):
+        z_from, _ = on_line(dz, 0)
+        block = z_from * chips + chip
+        if dz:
+            arrived(proj_all.at[block], line_recv.at[z_from])
+            for dx in range(1, chips):
+                row_copy(dz, dx).start()
+            if dz < AHEAD:
+                send_grads(dz)
+            accumulate(block, proj_all[block])
+        else:
+            accumulate(block, proj_ref[...])
+    for dz in range(LINE):
+        z_from, _ = on_line(dz, 0)
+        for dx in range(1, chips):
+            block = z_from * chips + lax.rem(chip + dx, chips)
+            arrived(proj_all.at[block], row_recv.at[block])
+            accumulate(block, proj_all[block])
+    acc_copy().start()
+    arrived(acc_in, acc_recv)
+    summed = jnp.transpose(acc[0] + acc_in[...]).astype(jnp.bfloat16)
+    coords[...] = summed.reshape(coords.shape)
+    each_coords_copy(lambda copy: copy.start())
+    for q in range(parts):
+        chip_to, own_block = coords_place(q)
+
+        @pl.when(chip_to == chip)
+        def _():
+            coords_all[slot, own_block] = coords[q]
+
+    for step in range(plane):
         source = in_plane(step)
-        arrived(coords_all.at[source], coords_recv.at[source])
+        for block in range(LINE):
+            if step:
+                arrived(coords_all.at[source, block], coords_recv.at[source, block])
+            else:
+                @pl.when(lax.div(block * chips + chip, parts) != tp)
+                def _():
+                    arrived(coords_all.at[source, block], coords_recv.at[source, block])
 
     def multiply(i):
         own_copy(i).wait()
         for step in range(1, plane):
             source = in_plane(step)
             arrived(grads.at[source, i], grad_recv.at[source, i])
-        total = jnp.dot(coords_all[0], grads[0, i], preferred_element_type=jnp.float32)
-        for source in range(1, plane):
-            total += jnp.dot(
-                coords_all[source], grads[source, i], preferred_element_type=jnp.float32
-            )
+        total = 0.0
+        for source in range(plane):
+            ranks = coords_all[source].reshape(LINE * CORES * rows, -1)
+            total += jnp.dot(ranks, grads[source, i], preferred_element_type=jnp.float32)
         total = total.astype(jnp.bfloat16)
         for block in range(LINE * CORES):
             partial[block, i] = total[block * rows : (block + 1) * rows]
@@ -164,8 +287,15 @@
     def _(i):
         adam(i)
 
-    for step in range(1, plane):
-        coords_copy(step).wait_send()
+    for dz in range(1, LINE):
+        line_copy(dz).wait_send()
+    for dz in range(LINE):
+        for dx in range(1, chips):
+            row_copy(dz, dx).wait_send()
+    for block in range(blocks):
+        act_copy(block).wait_send()
+    acc_copy().wait_send()
+    each_coords_copy(lambda copy: copy.wait_send())
 
     @pl.loop(0, CHUNKS)
     def _(i):
@@ -175,13 +305,19 @@
             part_copy(index, i).wait_send()
 
 
-def reduced(coords, grad_output, first_moment, second_moment):
-    chips, share, tokens = coords.shape
-    plane = chips * CORES
+def reduced(activations, proj_block, grad_output, first_moment, second_moment):
+    tps = lax.axis_size("tp")
+    plane = lax.axis_size("fsdp") // LINE
+    blocks = plane * LINE // CORES
+    tokens = activations.shape[0]
+    depth, ranks = proj_block.shape
     rows, columns = first_moment.shape
+    parts = ranks // (CORES * rows)
     width = columns // CORES // CHUNKS
     peers = LINE * CORES - 1
+    dma = pltpu.SemaphoreType.DMA
     vmem = pl.BlockSpec(memory_space=pltpu.VMEM)
+    hbm = pl.BlockSpec(memory_space=pl.ANY)
     return pl.pallas_call(
         reduce_kernel,
         out_shape=(
@@ -189,26 +325,40 @@
             jax.ShapeDtypeStruct((rows, columns), jnp.float32),
             jax.ShapeDtypeStruct((rows, columns), jnp.bfloat16),
         ),
-        in_specs=[vmem, pl.BlockSpec(memory_space=pl.ANY), vmem, vmem],
+        in_specs=[hbm, vmem, hbm, vmem, vmem],
         out_specs=(vmem, vmem, vmem),
         scratch_shapes=[
-            pltpu.VMEM((plane, share, tokens), jnp.bfloat16),
+            pltpu.VMEM((blocks, depth, ranks), jnp.bfloat16),
+            pltpu.VMEM((blocks, CORES, tokens, depth), jnp.bfloat16),
+            pltpu.VMEM((CORES, tokens, ranks), jnp.float32),
+            pltpu.VMEM((tokens, ranks), jnp.float32),
+            pltpu.VMEM((parts, CORES * rows, tokens), jnp.bfloat16),
+            pltpu.VMEM((plane, LINE, CORES * rows, tokens), jnp.bfloat16),
             pltpu.VMEM((plane, CHUNKS, tokens, width), jnp.bfloat16),
             pltpu.VMEM((LINE * CORES, CHUNKS, rows, width), jnp.bfloat16),
             pltpu.VMEM((CORES, LINE, CHUNKS, rows, width), jnp.bfloat16),
-            pltpu.SemaphoreType.DMA((plane - 1,)),
-            pltpu.SemaphoreType.DMA((plane,)),
-            pltpu.SemaphoreType.DMA((CHUNKS,)),
-            pltpu.SemaphoreType.DMA((plane - 1, CHUNKS)),
-            pltpu.SemaphoreType.DMA((plane, CHUNKS)),
-            pltpu.SemaphoreType.DMA((peers, CHUNKS)),
-            pltpu.SemaphoreType.DMA((CORES, LINE, CHUNKS)),
+            dma((LINE,)),
+            dma((LINE,)),
+            dma((plane // CORES, LINE)),
+            dma((blocks,)),
+            dma((blocks,)),
+            dma((blocks,)),
+            dma((blocks,)),
+            dma,
+            dma,
+            dma((parts, CORES * tps)),
+            dma((plane, LINE)),
+            dma((CHUNKS,)),
+            dma((plane - 1, CHUNKS)),
+            dma((plane, CHUNKS)),
+            dma((peers, CHUNKS)),
+            dma((CORES, LINE, CHUNKS)),
         ],
         compiler_params=pltpu.CompilerParams(
-            collective_id=0, has_side_effects=True, vmem_limit_bytes=58 * 2**20
+            collective_id=0, has_side_effects=True, vmem_limit_bytes=62 * 2**20
         ),
         name="reduce_and_step",
-    )(coords, grad_output, first_moment, second_moment)
+    )(activations, proj_block, grad_output, first_moment, second_moment)
 
 
 def update_kernel(projector_ref, direction_ref, out_ref):
@@ -239,18 +389,11 @@
     rank_width = projector.shape[1]
     tp_count = lax.axis_size("tp")
     tp_place = lax.axis_index("tp")
-    chips = lax.axis_size("fsdp") // (LINE * CORES)
     column_count = rank_width // tp_count
     proj_block = lax.dynamic_slice_in_dim(projector, tp_place * column_count, column_count, 1)
-    proj_all = lax.all_gather(proj_block, "fsdp", axis=0, tiled=True)
-    coords_block = lax.dot_general(
-        proj_all, activations, (((0,), (1,)), ((), ())), preferred_element_type=jnp.float32
-    ).astype(jnp.bfloat16)
-    coords = lax.all_gather(coords_block, "tp", axis=0, tiled=True)
-    tokens = coords.shape[1]
-    coords = coords.reshape(LINE, chips, -1, tokens).transpose(1, 0, 2, 3)
-    coords = coords.reshape(chips, rank_width // chips, tokens)
-    new_first, new_second, direction = reduced(coords, grad_output, first_moment, second_moment)
+    new_first, new_second, direction = reduced(
+        activations, proj_block, grad_output, first_moment, second_moment
+    )
     direction_all = lax.all_gather(direction, "fsdp", axis=0, tiled=True)
     return (new_first, new_second, back_projected(projector, direction_all))
 

time: 483 us -> 486 us (level)
  Pallas kernels: 216 us -> 315 us
  waiting for transfers between devices: 228 us -> 149 us
  blocking collectives: 9.15 us -> 0 us
  matrix products: 6.94 us -> 0 us
    pallas_call x1, Pallas kernels: 191 us -> 290 us  [reduced(): pl.pallas_call(reduce_kernel, out_shape=(jax.ShapeDtypeStruct((rows, colu...]
    all_gather x1 -> x0, waiting for transfers between devices: 79.2 us -> none  [body(): proj_all = lax.all_gather(proj_block, 'fsdp', axis=0, tiled=True)]
    all_gather x1 -> x0, blocking collectives: 9.15 us -> none  [body(): coords = lax.all_gather(coords_block, 'tp', axis=0, tiled=True)]
    dot_general x1 -> x0, matrix products: 6.94 us -> none  [body(): lax.dot_general(proj_all, activations, (((0,), (1,)), ((), ())), preferre...]
  transfers between devices with their start and end apart: 2 -> 1, of which waited for: 2 -> 1; matrix products, arithmetic and copies ran while one was open for 0% -> 0% of each run, Pallas kernels for 0% -> 0%
where the time goes in v2:
time: 486 us
  Pallas kernels  315 us (65%)
  waiting for transfers between devices  149 us (31%)
  between operations  14 us (3%)
  local copies, waits for them, and re-layouts  7.08 us (1%)
    pallas_call x1, Pallas kernels, reduced(): pl.pallas_call(reduce_kernel, out_shape=(jax.ShapeDtypeStruct((rows, colu...  290 us
    all_gather x1, waiting for transfers between devices, body(): direction_all = lax.all_gather(direction, 'fsdp', axis=0, tiled=True)  149 us
    pallas_call x1, Pallas kernels, back_projected(): pl.pallas_call(update_kernel, out_shape=jax.ShapeDtypeStruct((rows, colum...  25.4 us
  transfers between devices with their start and end apart: 1, of which 1 were waited for; matrix products, arithmetic and copies ran while one was open for 0% of the time, Pallas kernels for 0%

profile of v2, /device:TPU:0, one launch (start us, length us, event | category | flops | bytes accessed | tf_op | source)
XLA Modules:
  0.0 485.6 jit_solution(17642172377894692153)
XLA Ops:
  7.2 0.0 all-gather.2.cloned.1.call-start
  7.2 1.9 constant_dynamic-slice_fusion.proj_ref
  9.1 0.0 copy-start
  9.1 289.7 %reduce_and_step.1 = (f32[64,14336]{1,0:T(8,128)}, f32[64,14336]{1,0:T(8,128)}, bf16[64,14336]{1,0:T(8,128)(2,1)}) custom-call(bf16[256,8192]{1,0:T(8,128)(2,1)} %act_ref.1, bf16[512,512]{1,0:T(8,128)(2,1)} %constant_dynamic-slice_fusion.proj_ref, bf16[256,14336]{1,0:T(8,128)(2,1)} %grad_ref.1, f32[64,14336]{1,0:T(8,128)} %first_ref.1, f32[64,14336]{1,0:T(8,128)} %second_ref.1), custom_call_target="tpu_custom_call" | custom-call | tf_op jit(solution)/shard_map/reduce_and_step/pallas_call | solution.py:321
  298.8 0.0 all-gather.2.cloned.1.call-update
  298.8 149.4 %all-gather.2.cloned.1.call-done.direction_ref = bf16[1024,14336]{1,0:T(8,128)(2,1)} async-done(((bf16[64,14336]{1,0:T(8,128)(2,1)}), bf16[1024,14336]{1,0:T(8,128)(2,1)}) %all-gather.2.cloned.1.call-update) | async-done | bytes 29360144 | tf_op jit(solution)/shard_map/all_gather | solution.py:397
  448.2 0.0 copy-done
  448.2 0.0 copy-start.2
  448.2 25.4 %back_project.1 = bf16[512,14336]{1,0:T(8,128)(2,1)} custom-call(bf16[512,1024]{1,0:T(8,128)(2,1)S(1)} %copy-done, bf16[1024,14336]{1,0:T(8,128)(2,1)} %all-gather.2.cloned.1.call-done.direction_ref), custom_call_target="tpu_custom_call" | custom-call | tf_op jit(solution)/shard_map/back_project/pallas_call | solution.py:374
  473.6 0.0 copy-done.2
  473.6 0.0 copy-start.1
  473.6 1.9 copy.10
  475.4 1.5 copy-done.1
  476.9 1.8 copy.11
Async XLA Ops:
  7.2 441.0 %all-gather.2.cloned.1.call-start = ((), (), s32[]{:S(2)}) async-start(), calls=%async_computation | async-start | bytes 31195136 | tf_op jit(solution)/shard_map/all_gather | solution.py:397
  9.1 439.1 %copy-start = (bf16[512,1024]{1,0:T(8,128)(2,1)S(1)}, bf16[512,1024]{1,0:T(8,128)(2,1)}, u32[]{:S(2)}) copy-start(bf16[512,1024]{1,0:T(8,128)(2,1)} %projector_ref.1) | copy-start | bytes 3145732
  448.2 25.4 %copy-start.2 = (f32[64,14336]{1,0:T(8,128)S(1)}, f32[64,14336]{1,0:T(8,128)}, u32[]{:S(2)}) copy-start(f32[64,14336]{1,0:T(8,128)} %get-tuple-element.12) | copy-start | bytes 11010052
  473.6 3.4 copy-start.1
Sparse Core Ops, SparseCore 0:
  298.9 149.1 all-gather.1

commit v3 on v2

--- a/solution.py
+++ b/solution.py
@@ -21,9 +21,9 @@
 def reduce_kernel(
     act_ref, proj_ref, grad_ref, first_ref, second_ref,
     new_first_ref, new_second_ref, direction_ref,
-    proj_all, acts, acc, acc_in, coords, coords_all, grads, partial, landed,
+    proj_all, acts, acc, acc_in, coords, coords_all, grads, partial, landed, relay,
     line_send, line_recv, row_send, row_recv, act_sem, act_send, act_recv, acc_send, acc_recv,
-    coords_send, coords_recv, own_sem, grad_send, grad_recv, part_send, part_recv,
+    coords_send, coords_recv, own_sem, grad_send, grad_recv, part_send, part_recv, relay_recv,
 ):
     plane = grads.shape[0]
     chips = plane // CORES
@@ -47,6 +47,10 @@
     def on_line(dz, dc):
         return lax.rem(z + dz, LINE), lax.rem(core + dc, CORES)
 
+    low = z < LINE // 2
+    middle = jnp.logical_or(z == 1, z == 2)
+    partner = jnp.where(low, 1 - z, 5 - z)
+    far = jnp.where(low, LINE // 2, 0)
     line_peers = [(dz, dc) for dz in range(LINE) for dc in range(CORES) if dz or dc]
 
     def device(z_to, slot_to, dt=0):
@@ -70,24 +74,32 @@
     def arrived(ref, sem):
         pltpu.make_async_copy(ref, ref, sem).wait()
 
-    def line_copy(dz):
-        z_to, _ = on_line(dz, 0)
-        return pltpu.make_async_remote_copy(
-            src_ref=proj_ref,
-            dst_ref=proj_all.at[z * chips + chip],
-            send_sem=line_send.at[dz],
-            recv_sem=line_recv.at[z],
-            device_id=device(z_to, slot),
-            device_id_type=MESH,
-        )
-
-    def row_copy(dz, dx):
-        z_from, _ = on_line(dz, 0)
+    def line_source(k, way):
+        return z + k if way else z - k
+
+    def line_valid(k, way):
+        return z + k < LINE if way else z >= k
+
+    def line_next(k, way):
+        return jnp.logical_and(line_valid(k, way), z > 0 if way else z < LINE - 1)
+
+    def line_copy(k, way):
+        block = line_source(k, way) * chips + chip
+        return pltpu.make_async_remote_copy(
+            src_ref=proj_all.at[block] if k else proj_ref,
+            dst_ref=proj_all.at[block],
+            send_sem=line_send.at[way, k],
+            recv_sem=line_recv.at[line_source(k, way)],
+            device_id=device(z - 1 if way else z + 1, slot),
+            device_id_type=MESH,
+        )
+
+    def row_copy(z_from, dx, own=False):
         block = z_from * chips + chip
         return pltpu.make_async_remote_copy(
-            src_ref=proj_all.at[block] if dz else proj_ref,
+            src_ref=proj_ref if own else proj_all.at[block],
             dst_ref=proj_all.at[block],
-            send_sem=row_send.at[dx, dz],
+            send_sem=row_send.at[dx, z_from],
             recv_sem=row_recv.at[block],
             device_id=device(z, lax.rem(chip + dx, chips) * CORES + core),
             device_id_type=MESH,
@@ -165,15 +177,36 @@
         )
 
     def part_copy(index, i):
-        z_to, core_to = on_line(*line_peers[index])
+        if index == 0:
+            z_to, core_to = z, 1 - core
+        else:
+            z_to, core_to = partner, index - 1
         return pltpu.make_async_remote_copy(
             src_ref=partial.at[z_to * CORES + core_to, i],
-            dst_ref=landed.at[core, z, i],
+            dst_ref=landed.at[core, min(index, 1), i],
             send_sem=part_send.at[index, i],
-            recv_sem=part_recv.at[core, z, i],
+            recv_sem=part_recv.at[core, min(index, 1), i],
             device_id=device(z_to, chip * CORES + core_to),
             device_id_type=MESH,
         )
+
+    def far_copy(f, core_to, i, relayed):
+        if relayed:
+            dst_ref, recv_sem = landed.at[core, 2, i], part_recv.at[core, 2, i]
+            target = device(far + f, chip * CORES + core_to)
+        else:
+            dst_ref, recv_sem = relay.at[f, core_to, i], relay_recv.at[f, core_to, i]
+            target = device(partner, slot)
+        return pltpu.make_async_remote_copy(
+            src_ref=partial.at[(far + f) * CORES + core_to, i],
+            dst_ref=dst_ref,
+            send_sem=part_send.at[3 + f * CORES + core_to, i],
+            recv_sem=recv_sem,
+            device_id=target,
+            device_id_type=MESH,
+        )
+
+    far_blocks = [(f, core_to) for f in range(LINE // 2) for core_to in range(CORES)]
 
     def send_grads(i):
         own_copy(i).start()
@@ -181,14 +214,16 @@
             grad_copy(step, i).start()
 
     blocks = acts.shape[0]
-    for dz in range(1, LINE):
-        line_copy(dz).start()
+    for way in range(2):
+        @pl.when(line_next(0, way))
+        def _():
+            line_copy(0, way).start()
+
     for dx in range(1, chips):
-        row_copy(0, dx).start()
+        row_copy(z, dx, True).start()
     for block in range(blocks):
         act_own(block).start()
         act_copy(block).start()
-    send_grads(0)
     acc[...] = jnp.zeros_like(acc)
 
     def accumulate(block, features):
@@ -198,18 +233,28 @@
         both = acts[block].reshape(CORES * tokens, depth)
         acc[...] += jnp.dot(both, features, preferred_element_type=jnp.float32).reshape(acc.shape)
 
-    for dz in range(LINE):
-        z_from, _ = on_line(dz, 0)
-        block = z_from * chips + chip
-        if dz:
-            arrived(proj_all.at[block], line_recv.at[z_from])
-            for dx in range(1, chips):
-                row_copy(dz, dx).start()
-            if dz < AHEAD:
-                send_grads(dz)
-            accumulate(block, proj_all[block])
-        else:
-            accumulate(block, proj_ref[...])
+    accumulate(z * chips + chip, proj_ref[...])
+    for k in range(1, LINE):
+        for way in range(2):
+            @pl.when(line_valid(k, way))
+            def _():
+                z_from = line_source(k, way)
+                arrived(proj_all.at[z_from * chips + chip], line_recv.at[z_from])
+                for dx in range(1, chips):
+                    row_copy(z_from, dx).start()
+
+            if k < LINE - 1:
+                @pl.when(line_next(k, way))
+                def _():
+                    line_copy(k, way).start()
+
+        for way in range(2):
+            @pl.when(line_valid(k, way))
+            def _():
+                block = line_source(k, way) * chips + chip
+                accumulate(block, proj_all[block])
+
+    send_grads(0)
     for dz in range(LINE):
         z_from, _ = on_line(dz, 0)
         for dx in range(1, chips):
@@ -217,6 +262,7 @@
             arrived(proj_all.at[block], row_recv.at[block])
             accumulate(block, proj_all[block])
     acc_copy().start()
+    send_grads(1)
     arrived(acc_in, acc_recv)
     summed = jnp.transpose(acc[0] + acc_in[...]).astype(jnp.bfloat16)
     coords[...] = summed.reshape(coords.shape)
@@ -237,6 +283,9 @@
                 @pl.when(lax.div(block * chips + chip, parts) != tp)
                 def _():
                     arrived(coords_all.at[source, block], coords_recv.at[source, block])
+
+    for i in range(2, AHEAD):
+        send_grads(i)
 
     def multiply(i):
         own_copy(i).wait()
@@ -250,18 +299,34 @@
         total = total.astype(jnp.bfloat16)
         for block in range(LINE * CORES):
             partial[block, i] = total[block * rows : (block + 1) * rows]
-        for index in range(len(line_peers)):
+        for index in range(1 + CORES):
             part_copy(index, i).start()
-        landed[core, z, i] = partial[z * CORES + core, i]
+        landed[core, 0, i] = partial[z * CORES + core, i]
+
+        @pl.when(jnp.logical_not(middle))
+        def _():
+            for f, core_to in far_blocks:
+                far_copy(f, core_to, i, False).start()
+
+    def pass_on(i):
+        @pl.when(middle)
+        def _():
+            for f, core_to in far_blocks:
+                arrived(relay.at[f, core_to, i], relay_recv.at[f, core_to, i])
+                block = (far + f) * CORES + core_to
+                both = partial[block, i].astype(jnp.float32) + relay[f, core_to, i].astype(jnp.float32)
+                partial[block, i] = both.astype(jnp.bfloat16)
+                far_copy(f, core_to, i, True).start()
 
     def adam(i):
-        for dz, dc in line_peers:
-            z_from, core_from = on_line(dz, dc)
-            arrived(landed.at[core_from, z_from, i], part_recv.at[core_from, z_from, i])
+        for dc in range(CORES):
+            core_from = lax.rem(core + dc, CORES)
+            for place in range(0 if dc else 1, 3):
+                arrived(landed.at[core_from, place, i], part_recv.at[core_from, place, i])
         for side in range(CORES):
             lowrank = landed[side, 0, i].astype(jnp.float32)
-            for z_from in range(1, LINE):
-                lowrank += landed[side, z_from, i].astype(jnp.float32)
+            for place in range(1, 3):
+                lowrank += landed[side, place, i].astype(jnp.float32)
             columns = pl.ds(pl.multiple_of(side * half + i * width, 128), width)
             new_first = 0.9 * first_ref[:, columns] + 0.1 * lowrank
             new_second = 0.99 * second_ref[:, columns] + 0.01 * lowrank * lowrank
@@ -279,19 +344,29 @@
 
         multiply(i)
 
+        @pl.when(i >= 1)
+        def _():
+            pass_on(i - 1)
+
         @pl.when(i >= LAG)
         def _():
             adam(i - LAG)
+
+    pass_on(CHUNKS - 1)
 
     @pl.loop(CHUNKS - LAG, CHUNKS)
     def _(i):
         adam(i)
 
-    for dz in range(1, LINE):
-        line_copy(dz).wait_send()
-    for dz in range(LINE):
+    for k in range(LINE - 1):
+        for way in range(2):
+            @pl.when(line_next(k, way))
+            def _():
+                line_copy(k, way).wait_send()
+
+    for z_from in range(LINE):
         for dx in range(1, chips):
-            row_copy(dz, dx).wait_send()
+            row_copy(z_from, dx).wait_send()
     for block in range(blocks):
         act_copy(block).wait_send()
     acc_copy().wait_send()
@@ -301,8 +376,10 @@
     def _(i):
         for step in range(1, plane):
             grad_copy(step, i).wait_send()
-        for index in range(len(line_peers)):
+        for index in range(1 + CORES):
             part_copy(index, i).wait_send()
+        for f, core_to in far_blocks:
+            far_copy(f, core_to, i, True).wait_send()
 
 
 def reduced(activations, proj_block, grad_output, first_moment, second_moment):
@@ -336,8 +413,9 @@
             pltpu.VMEM((plane, LINE, CORES * rows, tokens), jnp.bfloat16),
             pltpu.VMEM((plane, CHUNKS, tokens, width), jnp.bfloat16),
             pltpu.VMEM((LINE * CORES, CHUNKS, rows, width), jnp.bfloat16),
-            pltpu.VMEM((CORES, LINE, CHUNKS, rows, width), jnp.bfloat16),
-            dma((LINE,)),
+            pltpu.VMEM((CORES, 3, CHUNKS, rows, width), jnp.bfloat16),
+            pltpu.VMEM((LINE // 2, CORES, CHUNKS, rows, width), jnp.bfloat16),
+            dma((2, LINE - 1)),
             dma((LINE,)),
             dma((plane // CORES, LINE)),
             dma((blocks,)),
@@ -352,7 +430,8 @@
             dma((plane - 1, CHUNKS)),
             dma((plane, CHUNKS)),
             dma((peers, CHUNKS)),
-            dma((CORES, LINE, CHUNKS)),
+            dma((CORES, 3, CHUNKS)),
+            dma((LINE // 2, CORES, CHUNKS)),
         ],
         compiler_params=pltpu.CompilerParams(
             collective_id=0, has_side_effects=True, vmem_limit_bytes=62 * 2**20

time: 486 us -> 441 us (0.907)
  Pallas kernels: 315 us -> 270 us
    pallas_call x1, Pallas kernels: 290 us -> 245 us  [reduced(): pl.pallas_call(reduce_kernel, out_shape=(jax.ShapeDtypeStruct((rows, colu...]
where the time goes in v3:
time: 441 us
  Pallas kernels  270 us (61%)
  waiting for transfers between devices  149 us (34%)
  between operations  14 us (3%)
  local copies, waits for them, and re-layouts  7.08 us (2%)
    pallas_call x1, Pallas kernels, reduced(): pl.pallas_call(reduce_kernel, out_shape=(jax.ShapeDtypeStruct((rows, colu...  245 us
    all_gather x1, waiting for transfers between devices, body(): direction_all = lax.all_gather(direction, 'fsdp', axis=0, tiled=True)  149 us
    pallas_call x1, Pallas kernels, back_projected(): pl.pallas_call(update_kernel, out_shape=jax.ShapeDtypeStruct((rows, colum...  25.4 us
  transfers between devices with their start and end apart: 1, of which 1 were waited for; matrix products, arithmetic and copies ran while one was open for 0% of the time, Pallas kernels for 0%

profile of v3, /device:TPU:0, one launch (start us, length us, event | category | flops | bytes accessed | tf_op | source)
XLA Modules:
  0.0 440.5 jit_solution(4497815980336272455)
XLA Ops:
  7.2 0.0 all-gather.2.cloned.1.call-start
  7.2 1.9 constant_dynamic-slice_fusion.proj_ref
  9.1 0.0 copy-start
  9.1 245.0 %reduce_and_step.1 = (f32[64,14336]{1,0:T(8,128)}, f32[64,14336]{1,0:T(8,128)}, bf16[64,14336]{1,0:T(8,128)(2,1)}) custom-call(bf16[256,8192]{1,0:T(8,128)(2,1)} %act_ref.1, bf16[512,512]{1,0:T(8,128)(2,1)} %constant_dynamic-slice_fusion.proj_ref, bf16[256,14336]{1,0:T(8,128)(2,1)} %grad_ref.1, f32[64,14336]{1,0:T(8,128)} %first_ref.1, f32[64,14336]{1,0:T(8,128)} %second_ref.1), custom_call_target="tpu_custom_call" | custom-call | tf_op jit(solution)/shard_map/reduce_and_step/pallas_call | solution.py:398
  254.1 0.0 all-gather.2.cloned.1.call-update
  254.2 148.9 %all-gather.2.cloned.1.call-done.direction_ref = bf16[1024,14336]{1,0:T(8,128)(2,1)} async-done(((bf16[64,14336]{1,0:T(8,128)(2,1)}), bf16[1024,14336]{1,0:T(8,128)(2,1)}) %all-gather.2.cloned.1.call-update) | async-done | bytes 29360144 | tf_op jit(solution)/shard_map/all_gather | solution.py:476
  403.1 0.0 copy-done
  403.1 0.0 copy-start.2
  403.1 25.4 %back_project.1 = bf16[512,14336]{1,0:T(8,128)(2,1)} custom-call(bf16[512,1024]{1,0:T(8,128)(2,1)S(1)} %copy-done, bf16[1024,14336]{1,0:T(8,128)(2,1)} %all-gather.2.cloned.1.call-done.direction_ref), custom_call_target="tpu_custom_call" | custom-call | tf_op jit(solution)/shard_map/back_project/pallas_call | solution.py:453
  428.5 0.0 copy-done.2
  428.5 0.0 copy-start.1
  428.5 1.9 copy.10
  430.3 1.5 copy-done.1
  431.8 1.8 copy.11
Async XLA Ops:
  7.2 395.9 %all-gather.2.cloned.1.call-start = ((), (), s32[]{:S(2)}) async-start(), calls=%async_computation | async-start | bytes 31195136 | tf_op jit(solution)/shard_map/all_gather | solution.py:476
  9.1 394.0 %copy-start = (bf16[512,1024]{1,0:T(8,128)(2,1)S(1)}, bf16[512,1024]{1,0:T(8,128)(2,1)}, u32[]{:S(2)}) copy-start(bf16[512,1024]{1,0:T(8,128)(2,1)} %projector_ref.1) | copy-start | bytes 3145732
  403.1 25.4 %copy-start.2 = (f32[64,14336]{1,0:T(8,128)S(1)}, f32[64,14336]{1,0:T(8,128)}, u32[]{:S(2)}) copy-start(f32[64,14336]{1,0:T(8,128)} %get-tuple-element.12) | copy-start | bytes 11010052
  428.5 3.4 copy-start.1
Sparse Core Ops, SparseCore 0:
  254.3 148.7 all-gather.1

commit v4 on v3

--- a/solution.py
+++ b/solution.py
@@ -14,15 +14,16 @@
 LINE = 4
 CORES = 2
 CHUNKS = 14
-AHEAD = 4
+AHEAD = 6
+REACH = 2
 LAG = 4
 
 
 def reduce_kernel(
     act_ref, proj_ref, grad_ref, first_ref, second_ref,
-    new_first_ref, new_second_ref, direction_ref,
+    lowrank_ref, direction_ref,
     proj_all, acts, acc, acc_in, coords, coords_all, grads, partial, landed, relay,
-    line_send, line_recv, row_send, row_recv, act_sem, act_send, act_recv, acc_send, acc_recv,
+    line_send, line_recv, cross_send, row_send, row_recv, act_sem, act_send, act_recv, acc_send, acc_recv,
     coords_send, coords_recv, own_sem, grad_send, grad_recv, part_send, part_recv, relay_recv,
 ):
     plane = grads.shape[0]
@@ -105,6 +106,17 @@
             device_id_type=MESH,
         )
 
+    def cross_copy(k, way, dx):
+        block = line_source(k, way) * chips + lax.rem(chip + dx, chips)
+        return pltpu.make_async_remote_copy(
+            src_ref=proj_all.at[block],
+            dst_ref=proj_all.at[block],
+            send_sem=cross_send.at[way, k, dx],
+            recv_sem=row_recv.at[block],
+            device_id=device(z - 1 if way else z + 1, slot),
+            device_id_type=MESH,
+        )
+
     def act_columns(block, side):
         return act_ref.at[:, pl.ds(pl.multiple_of((block * CORES + side) * depth, 128), depth)]
 
@@ -233,15 +245,30 @@
         both = acts[block].reshape(CORES * tokens, depth)
         acc[...] += jnp.dot(both, features, preferred_element_type=jnp.float32).reshape(acc.shape)
 
+    def take_beside(k, way):
+        for dx in range(1, chips):
+            block = line_source(k, way) * chips + lax.rem(chip + dx, chips)
+            arrived(proj_all.at[block], row_recv.at[block])
+            if k < REACH:
+                for onward in range(2) if k == 0 else (way,):
+                    @pl.when(line_next(k, onward))
+                    def _():
+                        cross_copy(k, onward, dx).start()
+
+            accumulate(block, proj_all[block])
+
     accumulate(z * chips + chip, proj_ref[...])
+    take_beside(0, 0)
+    send_grads(0)
     for k in range(1, LINE):
         for way in range(2):
             @pl.when(line_valid(k, way))
             def _():
                 z_from = line_source(k, way)
                 arrived(proj_all.at[z_from * chips + chip], line_recv.at[z_from])
-                for dx in range(1, chips):
-                    row_copy(z_from, dx).start()
+                if k > REACH:
+                    for dx in range(1, chips):
+                        row_copy(z_from, dx).start()
 
             if k < LINE - 1:
                 @pl.when(line_next(k, way))
@@ -251,18 +278,21 @@
         for way in range(2):
             @pl.when(line_valid(k, way))
             def _():
+                if k <= REACH:
+                    take_beside(k, way)
                 block = line_source(k, way) * chips + chip
                 accumulate(block, proj_all[block])
 
-    send_grads(0)
-    for dz in range(LINE):
-        z_from, _ = on_line(dz, 0)
-        for dx in range(1, chips):
-            block = z_from * chips + lax.rem(chip + dx, chips)
-            arrived(proj_all.at[block], row_recv.at[block])
-            accumulate(block, proj_all[block])
+        if k < LINE - 1:
+            send_grads(k)
+    for k in range(REACH + 1, LINE):
+        for way in range(2):
+            @pl.when(line_valid(k, way))
+            def _():
+                take_beside(k, way)
+
+    send_grads(LINE - 1)
     acc_copy().start()
-    send_grads(1)
     arrived(acc_in, acc_recv)
     summed = jnp.transpose(acc[0] + acc_in[...]).astype(jnp.bfloat16)
     coords[...] = summed.reshape(coords.shape)
@@ -284,7 +314,7 @@
                 def _():
                     arrived(coords_all.at[source, block], coords_recv.at[source, block])
 
-    for i in range(2, AHEAD):
+    for i in range(LINE, AHEAD):
         send_grads(i)
 
     def multiply(i):
@@ -330,8 +360,7 @@
             columns = pl.ds(pl.multiple_of(side * half + i * width, 128), width)
             new_first = 0.9 * first_ref[:, columns] + 0.1 * lowrank
             new_second = 0.99 * second_ref[:, columns] + 0.01 * lowrank * lowrank
-            new_first_ref[:, columns] = new_first
-            new_second_ref[:, columns] = new_second
+            lowrank_ref[:, columns] = lowrank
             direction_ref[:, columns] = (
                 new_first / first_fix / (jnp.sqrt(new_second / second_fix) + 1e-08)
             ).astype(jnp.bfloat16)
@@ -364,9 +393,22 @@
             def _():
                 line_copy(k, way).wait_send()
 
-    for z_from in range(LINE):
-        for dx in range(1, chips):
-            row_copy(z_from, dx).wait_send()
+    for dx in range(1, chips):
+        row_copy(z, dx, True).wait_send()
+    for k in range(REACH):
+        for way in range(2):
+            @pl.when(line_next(k, way))
+            def _():
+                for dx in range(1, chips):
+                    cross_copy(k, way, dx).wait_send()
+
+    for k in range(REACH + 1, LINE):
+        for way in range(2):
+            @pl.when(line_valid(k, way))
+            def _():
+                for dx in range(1, chips):
+                    row_copy(line_source(k, way), dx).wait_send()
+
     for block in range(blocks):
         act_copy(block).wait_send()
     acc_copy().wait_send()
@@ -399,11 +441,10 @@
         reduce_kernel,
         out_shape=(
             jax.ShapeDtypeStruct((rows, columns), jnp.float32),
-            jax.ShapeDtypeStruct((rows, columns), jnp.float32),
             jax.ShapeDtypeStruct((rows, columns), jnp.bfloat16),
         ),
         in_specs=[hbm, vmem, hbm, vmem, vmem],
-        out_specs=(vmem, vmem, vmem),
+        out_specs=(vmem, vmem),
         scratch_shapes=[
             pltpu.VMEM((blocks, depth, ranks), jnp.bfloat16),
             pltpu.VMEM((blocks, CORES, tokens, depth), jnp.bfloat16),
@@ -417,6 +458,7 @@
             pltpu.VMEM((LINE // 2, CORES, CHUNKS, rows, width), jnp.bfloat16),
             dma((2, LINE - 1)),
             dma((LINE,)),
+            dma((2, REACH, plane // CORES)),
             dma((plane // CORES, LINE)),
             dma((blocks,)),
             dma((blocks,)),
@@ -470,9 +512,11 @@
     tp_place = lax.axis_index("tp")
     column_count = rank_width // tp_count
     proj_block = lax.dynamic_slice_in_dim(projector, tp_place * column_count, column_count, 1)
-    new_first, new_second, direction = reduced(
+    lowrank, direction = reduced(
         activations, proj_block, grad_output, first_moment, second_moment
     )
+    new_first = 0.9 * first_moment + 0.1 * lowrank
+    new_second = 0.99 * second_moment + 0.01 * lowrank * lowrank
     direction_all = lax.all_gather(direction, "fsdp", axis=0, tiled=True)
     return (new_first, new_second, back_projected(projector, direction_all))
 

time: 441 us -> 425 us (0.964)
  Pallas kernels: 270 us -> 259 us
  waiting for transfers between devices: 149 us -> 140 us
  other arithmetic: 0 us -> 8.99 us
  local copies, waits for them, and re-layouts: 7.08 us -> 1.88 us
    pallas_call x1, Pallas kernels: 245 us -> 233 us  [reduced(): pl.pallas_call(reduce_kernel, out_shape=(jax.ShapeDtypeStruct((rows, colu...]
    add x0 -> x1, other arithmetic: none -> 8.99 us  [body(): new_second = 0.99 * second_moment + 0.01 * lowrank * lowrank]
    all_gather x1, waiting for transfers between devices: 149 us -> 140 us  [body(): direction_all = lax.all_gather(direction, 'fsdp', axis=0, tiled=True)]
    unnamed x8 -> x2, local copies, waits for them, and re-layouts: 5.21 us -> 0.01 us
  transfers between devices with their start and end apart: 1 -> 1, of which waited for: 1 -> 1; matrix products, arithmetic and copies ran while one was open for 0% -> 2% of each run, Pallas kernels for 0% -> 0%
where the time goes in v4:
time: 425 us; the launch traced here: 424 us
  Pallas kernels  259 us (61%)
  waiting for transfers between devices  140 us (33%)
  between operations  14 us (3%)
  other arithmetic  8.99 us (2%)
    pallas_call x1, Pallas kernels, reduced(): pl.pallas_call(reduce_kernel, out_shape=(jax.ShapeDtypeStruct((rows, colu...  233 us
    all_gather x1, waiting for transfers between devices, body(): direction_all = lax.all_gather(direction, 'fsdp', axis=0, tiled=True)  140 us
    pallas_call x1, Pallas kernels, back_projected(): pl.pallas_call(update_kernel, out_shape=jax.ShapeDtypeStruct((rows, colum...  25.2 us
    add x1, other arithmetic, body(): new_second = 0.99 * second_moment + 0.01 * lowrank * lowrank  8.99 us
  transfers between devices with their start and end apart: 1, of which 1 were waited for; matrix products, arithmetic and copies ran while one was open for 2% of the time, Pallas kernels for 0%

profile of v4, /device:TPU:0, one launch (start us, length us, event | category | flops | bytes accessed | tf_op | source)
XLA Modules:
  0.0 424.0 jit_solution(17864297596960011256)
XLA Ops:
  7.2 0.0 all-gather.2.cloned.1.call-start
  7.2 1.9 constant_dynamic-slice_fusion.proj_ref
  9.1 233.4 %reduce_and_step.1 = (f32[64,14336]{1,0:T(8,128)}, bf16[64,14336]{1,0:T(8,128)(2,1)}) custom-call(bf16[256,8192]{1,0:T(8,128)(2,1)} %act_ref.1, bf16[512,512]{1,0:T(8,128)(2,1)} %constant_dynamic-slice_fusion.proj_ref, bf16[256,14336]{1,0:T(8,128)(2,1)} %grad_ref.1, f32[64,14336]{1,0:T(8,128)} %first_ref.1, f32[64,14336]{1,0:T(8,128)} %second_ref.1), custom_call_target="tpu_custom_call" | custom-call | tf_op jit(solution)/shard_map/reduce_and_step/pallas_call | solution.py:440
  242.5 0.0 all-gather.2.cloned.1.call-update
  242.6 0.0 copy-start
  242.6 9.0 %fusion = (f32[64,14336]{1,0:T(8,128)}, f32[64,14336]{1,0:T(8,128)}) fusion(f32[64,14336]{1,0:T(8,128)} %get-tuple-element.5, f32[64,14336]{1,0:T(8,128)} %second_ref.1, f32[64,14336]{1,0:T(8,128)} %first_ref.1), kind=kLoop, calls=%fused_computation.1 | loop fusion | flops 6422528 | bytes 18350080 | tf_op jit(solution)/shard_map/add | solution.py:519
  251.6 140.3 %all-gather.2.cloned.1.call-done.direction_ref = bf16[1024,14336]{1,0:T(8,128)(2,1)} async-done(((bf16[64,14336]{1,0:T(8,128)(2,1)}), bf16[1024,14336]{1,0:T(8,128)(2,1)}) %all-gather.2.cloned.1.call-update) | async-done | bytes 29360144 | tf_op jit(solution)/shard_map/all_gather | solution.py:520
  391.9 0.0 copy-done
  391.9 25.2 %back_project.1 = bf16[512,14336]{1,0:T(8,128)(2,1)} custom-call(bf16[512,1024]{1,0:T(8,128)(2,1)S(1)} %copy-done, bf16[1024,14336]{1,0:T(8,128)(2,1)} %all-gather.2.cloned.1.call-done.direction_ref), custom_call_target="tpu_custom_call" | custom-call | tf_op jit(solution)/shard_map/back_project/pallas_call | solution.py:495
Async XLA Ops:
  7.2 384.7 %all-gather.2.cloned.1.call-start = ((), (), s32[]{:S(2)}) async-start(), calls=%async_computation | async-start | bytes 31195136 | tf_op jit(solution)/shard_map/all_gather | solution.py:520
  242.6 149.3 %copy-start = (bf16[512,1024]{1,0:T(8,128)(2,1)S(1)}, bf16[512,1024]{1,0:T(8,128)(2,1)}, u32[]{:S(2)}) copy-start(bf16[512,1024]{1,0:T(8,128)(2,1)} %projector_ref.1) | copy-start | bytes 3145732
Sparse Core Ops, SparseCore 0:
  242.7 149.1 all-gather.1

commit v5 on v4

--- a/solution.py
+++ b/solution.py
@@ -20,9 +20,10 @@
 
 
 def reduce_kernel(
-    act_ref, proj_ref, grad_ref, first_ref, second_ref,
+    act_ref, proj_ref, grad_ref, first_in, second_in,
     lowrank_ref, direction_ref,
     proj_all, acts, acc, acc_in, coords, coords_all, grads, partial, landed, relay,
+    first_ref, second_ref, moment_sem,
     line_send, line_recv, cross_send, row_send, row_recv, act_sem, act_send, act_recv, acc_send, acc_recv,
     coords_send, coords_recv, own_sem, grad_send, grad_recv, part_send, part_recv, relay_recv,
 ):
@@ -257,7 +258,13 @@
 
             accumulate(block, proj_all[block])
 
+    moments = [
+        pltpu.make_async_copy(first_in, first_ref, moment_sem.at[0]),
+        pltpu.make_async_copy(second_in, second_ref, moment_sem.at[1]),
+    ]
     accumulate(z * chips + chip, proj_ref[...])
+    for copy in moments:
+        copy.start()
     take_beside(0, 0)
     send_grads(0)
     for k in range(1, LINE):
@@ -291,12 +298,12 @@
             def _():
                 take_beside(k, way)
 
-    send_grads(LINE - 1)
     acc_copy().start()
     arrived(acc_in, acc_recv)
     summed = jnp.transpose(acc[0] + acc_in[...]).astype(jnp.bfloat16)
     coords[...] = summed.reshape(coords.shape)
     each_coords_copy(lambda copy: copy.start())
+    send_grads(LINE - 1)
     for q in range(parts):
         chip_to, own_block = coords_place(q)
 
@@ -316,6 +323,9 @@
 
     for i in range(LINE, AHEAD):
         send_grads(i)
+
+    for copy in moments:
+        copy.wait()
 
     def multiply(i):
         own_copy(i).wait()
@@ -329,14 +339,14 @@
         total = total.astype(jnp.bfloat16)
         for block in range(LINE * CORES):
             partial[block, i] = total[block * rows : (block + 1) * rows]
+        @pl.when(jnp.logical_not(middle))
+        def _():
+            for f, core_to in far_blocks:
+                far_copy(f, core_to, i, False).start()
+
         for index in range(1 + CORES):
             part_copy(index, i).start()
         landed[core, 0, i] = partial[z * CORES + core, i]
-
-        @pl.when(jnp.logical_not(middle))
-        def _():
-            for f, core_to in far_blocks:
-                far_copy(f, core_to, i, False).start()
 
     def pass_on(i):
         @pl.when(middle)
@@ -443,7 +453,7 @@
             jax.ShapeDtypeStruct((rows, columns), jnp.float32),
             jax.ShapeDtypeStruct((rows, columns), jnp.bfloat16),
         ),
-        in_specs=[hbm, vmem, hbm, vmem, vmem],
+        in_specs=[hbm, vmem, hbm, hbm, hbm],
         out_specs=(vmem, vmem),
         scratch_shapes=[
             pltpu.VMEM((blocks, depth, ranks), jnp.bfloat16),
@@ -456,6 +466,9 @@
             pltpu.VMEM((LINE * CORES, CHUNKS, rows, width), jnp.bfloat16),
             pltpu.VMEM((CORES, 3, CHUNKS, rows, width), jnp.bfloat16),
             pltpu.VMEM((LINE // 2, CORES, CHUNKS, rows, width), jnp.bfloat16),
+            pltpu.VMEM((rows, columns), jnp.float32),
+            pltpu.VMEM((rows, columns), jnp.float32),
+            dma((2,)),
             dma((2, LINE - 1)),
             dma((LINE,)),
             dma((2, REACH, plane // CORES)),

time: 425 us -> 421 us (level)
  no operation moved by 1% of the time
where the time goes in v5:
time: 421 us
  Pallas kernels  255 us (61%)
  waiting for transfers between devices  141 us (33%)
  between operations  14 us (3%)
  other arithmetic  8.89 us (2%)
    pallas_call x1, Pallas kernels, reduced(): pl.pallas_call(reduce_kernel, out_shape=(jax.ShapeDtypeStruct((rows, colu...  230 us
    all_gather x1, waiting for transfers between devices, body(): direction_all = lax.all_gather(direction, 'fsdp', axis=0, tiled=True)  141 us
    pallas_call x1, Pallas kernels, back_projected(): pl.pallas_call(update_kernel, out_shape=jax.ShapeDtypeStruct((rows, colum...  25.2 us
    add x1, other arithmetic, body(): new_second = 0.99 * second_moment + 0.01 * lowrank * lowrank  8.89 us
  transfers between devices with their start and end apart: 1, of which 1 were waited for; matrix products, arithmetic and copies ran while one was open for 2% of the time, Pallas kernels for 0%

profile of v5, /device:TPU:0, one launch (start us, length us, event | category | flops | bytes accessed | tf_op | source)
XLA Modules:
  0.0 420.6 jit_solution(12037123072887418252)
XLA Ops:
  7.2 0.0 all-gather.2.cloned.1.call-start
  7.2 1.9 constant_dynamic-slice_fusion.proj_ref
  9.1 230.0 %reduce_and_step.1 = (f32[64,14336]{1,0:T(8,128)}, bf16[64,14336]{1,0:T(8,128)(2,1)}) custom-call(bf16[256,8192]{1,0:T(8,128)(2,1)} %act_ref.1, bf16[512,512]{1,0:T(8,128)(2,1)} %constant_dynamic-slice_fusion.proj_ref, bf16[256,14336]{1,0:T(8,128)(2,1)} %grad_ref.1, f32[64,14336]{1,0:T(8,128)} %first_in.1, f32[64,14336]{1,0:T(8,128)} %second_in.1), custom_call_target="tpu_custom_call" | custom-call | tf_op jit(solution)/shard_map/reduce_and_step/pallas_call | solution.py:450
  239.1 0.0 all-gather.2.cloned.1.call-update
  239.1 0.0 copy-start
  239.1 8.9 %fusion = (f32[64,14336]{1,0:T(8,128)}, f32[64,14336]{1,0:T(8,128)}) fusion(f32[64,14336]{1,0:T(8,128)} %get-tuple-element.5, f32[64,14336]{1,0:T(8,128)} %second_in.1, f32[64,14336]{1,0:T(8,128)} %first_in.1), kind=kLoop, calls=%fused_computation.1 | loop fusion | flops 6422528 | bytes 18350080 | tf_op jit(solution)/shard_map/add | solution.py:532
  248.0 140.5 %all-gather.2.cloned.1.call-done.direction_ref = bf16[1024,14336]{1,0:T(8,128)(2,1)} async-done(((bf16[64,14336]{1,0:T(8,128)(2,1)}), bf16[1024,14336]{1,0:T(8,128)(2,1)}) %all-gather.2.cloned.1.call-update) | async-done | bytes 29360144 | tf_op jit(solution)/shard_map/all_gather | solution.py:533
  388.6 0.0 copy-done
  388.6 25.2 %back_project.1 = bf16[512,14336]{1,0:T(8,128)(2,1)} custom-call(bf16[512,1024]{1,0:T(8,128)(2,1)S(1)} %copy-done, bf16[1024,14336]{1,0:T(8,128)(2,1)} %all-gather.2.cloned.1.call-done.direction_ref), custom_call_target="tpu_custom_call" | custom-call | tf_op jit(solution)/shard_map/back_project/pallas_call | solution.py:508
Async XLA Ops:
  7.2 381.4 %all-gather.2.cloned.1.call-start = ((), (), s32[]{:S(2)}) async-start(), calls=%async_computation | async-start | bytes 31195136 | tf_op jit(solution)/shard_map/all_gather | solution.py:533
  239.1 149.5 %copy-start = (bf16[512,1024]{1,0:T(8,128)(2,1)S(1)}, bf16[512,1024]{1,0:T(8,128)(2,1)}, u32[]{:S(2)}) copy-start(bf16[512,1024]{1,0:T(8,128)(2,1)} %projector_ref.1) | copy-start | bytes 3145732
Sparse Core Ops, SparseCore 0:
  239.2 149.2 all-gather.1
